TPU v7x, 32 devices: a whole 2x2x4 slice. The times are simulated.
32 devices in a mesh: grp: 2 (over x), wid: 4 (over y, core), hid: 4 (over z).
Axes of the slice: x: 2, y: 2, z: 4, core: 2. Of those that a mesh axis runs over, the one named last changes fastest.
Arguments:
- student_in: bfloat16 [512, 4096], P('wid'), may hold values from -6 to 6
- norm_gain: float32 [4096], replicated, may hold values from 0.1 to 1.9
- gate_weight: bfloat16 [4096, 7168], P(None, ('grp', 'hid')), may hold values from -0.09375 to 0.09375
- up_weight: bfloat16 [4096, 7168], P(None, ('grp', 'hid')), may hold values from -0.09375 to 0.09375
- down_weight: bfloat16 [7168, 4096], P(('grp', 'hid')), may hold values from -0.0625 to 0.0625
- projection: bfloat16 [4096, 4, 2048], P(None, None, ('grp', 'hid')), may hold values from -0.09375 to 0.09375
- teacher_in: bfloat16 [512, 8192], P(None, 'wid'), may hold values from -6 to 6
- teacher_gate: bfloat16 [8192, 14336], P('wid', ('grp', 'hid')), may hold values from -0.0625 to 0.0625
- teacher_up: bfloat16 [8192, 14336], P('wid', ('grp', 'hid')), may hold values from -0.0625 to 0.0625
- teacher_down: bfloat16 [14336, 8192], P(('grp', 'hid'), 'wid'), may hold values from -0.046875 to 0.046875
Outputs:
- grad_gate: bfloat16 [4096, 7168], P('wid', ('grp', 'hid'))
- grad_up: bfloat16 [4096, 7168], P('wid', ('grp', 'hid'))
- grad_down: bfloat16 [7168, 4096], P(('grp', 'hid'), 'wid')
- grad_proj: bfloat16 [4096, 4, 2048], P('wid', None, ('grp', 'hid'))
- input_grad: float32 [512, 4096], P('wid', ('grp', 'hid'))
All inputs are finite; a program needn't handle non-finite values.
Results may differ from a plain program's by a relative error of at most 0.02.
Values may be sent and summed in bfloat16 or wider, within the bound.
No kernel may reach another device: no remote copies, remote signals or barrier semaphores. Data moves between devices by JAX's collectives and lax.ppermute only.
A program may use at most 128 MiB of HBM per device.

v0:
```python
import math

import jax
import jax.numpy as jnp
from jax import lax
from jax.sharding import PartitionSpec as P


def shards(
    student_in,
    norm_gain,
    gate_weight,
    up_weight,
    down_weight,
    projection,
    teacher_in,
    teacher_gate,
    teacher_up,
    teacher_down,
):
    f32 = jnp.float32
    bf16 = jnp.bfloat16
    gate_part = jnp.dot(teacher_in, teacher_gate, preferred_element_type=f32)
    up_part = jnp.dot(teacher_in, teacher_up, preferred_element_type=f32)
    gate_rows, up_rows = (
        lax.psum_scatter(
            gate_part.astype(jnp.bfloat16), "wid", scatter_dimension=0, tiled=True
        ).astype(jnp.float32),
        lax.psum_scatter(
            up_part.astype(jnp.bfloat16), "wid", scatter_dimension=0, tiled=True
        ).astype(jnp.float32),
    )
    teacher_hidden = (gate_rows * jax.nn.sigmoid(gate_rows) * up_rows).astype(bf16)
    feature_part = jnp.dot(
        lax.all_gather(teacher_hidden, "wid", axis=0, tiled=True),
        teacher_down,
        preferred_element_type=f32,
    )
    target_cols = (
        lax.psum_scatter(
            feature_part.astype(jnp.bfloat16), ("grp", "hid"), scatter_dimension=1, tiled=True
        )
        .astype(jnp.float32)
        .astype(bf16)
    )
    target = lax.all_to_all(target_cols, "wid", split_axis=0, concat_axis=1, tiled=True)
    tokens_dev = student_in.shape[0]
    width = student_in.shape[1]
    total_tokens = tokens_dev * lax.axis_size("wid")
    inputs = student_in.astype(f32)
    inverse_rms = lax.rsqrt(jnp.mean(inputs * inputs, axis=-1, keepdims=True) + 1e-05)
    normed = (inputs * inverse_rms * norm_gain).astype(bf16)
    gate_sum = jnp.dot(normed, gate_weight, preferred_element_type=f32)
    up_sum = jnp.dot(normed, up_weight, preferred_element_type=f32)
    sigma = jax.nn.sigmoid(gate_sum)
    hidden = (gate_sum * sigma * up_sum).astype(bf16)
    branch = lax.psum(
        jnp.dot(hidden, down_weight, preferred_element_type=f32).astype(jnp.bfloat16),
        ("grp", "hid"),
    ).astype(jnp.float32)
    summed = (inputs + branch).astype(bf16)
    proj_local = projection.reshape(width, -1)
    features = jnp.dot(summed, proj_local, preferred_element_type=f32)
    feature_error = ((features - target.astype(f32)) / math.sqrt(total_tokens)).astype(bf16)
    feature_grad = lax.psum(
        jnp.dot(feature_error, proj_local.T, preferred_element_type=f32).astype(jnp.bfloat16),
        ("grp", "hid"),
    ).astype(jnp.float32)
    branch_grad = feature_grad.astype(bf16)
    hidden_grad = jnp.dot(branch_grad, down_weight.T, preferred_element_type=f32)
    gate_grad = (hidden_grad * up_sum * sigma * (1.0 + gate_sum * (1.0 - sigma))).astype(bf16)
    up_grad = (hidden_grad * gate_sum * sigma).astype(bf16)
    normed_grad = jnp.dot(gate_grad, gate_weight.T, preferred_element_type=f32) + jnp.dot(
        up_grad, up_weight.T, preferred_element_type=f32
    )
    share_cols = width // lax.axis_size(("grp", "hid"))
    offset = lax.axis_index(("grp", "hid")) * share_cols
    normed_total = lax.psum(normed_grad.astype(jnp.bfloat16), ("grp", "hid")).astype(jnp.float32)
    scaled = normed_total * norm_gain
    moment = jnp.mean(scaled * inputs, axis=-1, keepdims=True)
    whole = feature_grad + inverse_rms * (scaled - inputs * inverse_rms * inverse_rms * moment)
    input_grad = lax.dynamic_slice_in_dim(whole, offset, share_cols, 1)
    paired_grad = jnp.concatenate([gate_grad, up_grad], axis=1)
    normed_cols, summed_cols, branch_cols = (
        lax.all_to_all(normed, "wid", split_axis=1, concat_axis=0, tiled=True),
        lax.all_to_all(summed, "wid", split_axis=1, concat_axis=0, tiled=True),
        lax.all_to_all(branch_grad, "wid", split_axis=1, concat_axis=0, tiled=True),
    )
    hidden_all, paired_all, error_all = (
        lax.all_gather(hidden, "wid", axis=0, tiled=True),
        lax.all_gather(paired_grad, "wid", axis=0, tiled=True),
        lax.all_gather(feature_error, "wid", axis=0, tiled=True),
    )
    weight_grad = jnp.dot(normed_cols.T, paired_all, preferred_element_type=f32)
    hidden_cols = gate_grad.shape[1]
    grad_gate = weight_grad[:, :hidden_cols].astype(bf16)
    grad_up = weight_grad[:, hidden_cols:].astype(bf16)
    grad_down = jnp.dot(hidden_all.T, branch_cols, preferred_element_type=f32).astype(bf16)
    grad_proj = jnp.dot(summed_cols.T, error_all, preferred_element_type=f32).astype(bf16)
    grad_proj = grad_proj.reshape(summed_cols.shape[1], lax.axis_size("wid"), -1)
    return (grad_gate, grad_up, grad_down, grad_proj, input_grad)


def solution(mesh):
    in_specs = (
        P("wid", None),
        P(),
        P(None, ("grp", "hid")),
        P(None, ("grp", "hid")),
        P(("grp", "hid"), None),
        P(None, None, ("grp", "hid")),
        P(None, "wid"),
        P("wid", ("grp", "hid")),
        P("wid", ("grp", "hid")),
        P(("grp", "hid"), "wid"),
    )
    out_specs = (
        P("wid", ("grp", "hid")),
        P("wid", ("grp", "hid")),
        P(("grp", "hid"), "wid"),
        P("wid", None, ("grp", "hid")),
        P("wid", ("grp", "hid")),
    )
    return jax.shard_map(shards, mesh=mesh, in_specs=in_specs, out_specs=out_specs, check_vma=False)
```

profile of v0, /device:TPU:0, one launch (start us, length us, event | category | flops | bytes accessed | tf_op | source)
XLA Modules:
  0.0 493.3 jit_solution(5931833014790225035)
XLA Ops:
  8.8 8.1 %convolution_convert_fusion.4 = bf16[512,1792]{1,0:T(8,128)(2,1)} fusion(bf16[512,2048]{1,0:T(8,128)(2,1)S(1)} %copy-done, bf16[2048,1792]{1,0:T(8,128)(2,1)} %param.18), kind=kOutput, calls=%fused_computation.10 | convolution fusion | flops 3759013888 | bytes 11272192 | tf_op jit(solution)/shard_map/dot_general | solution.py:24
  17.0 8.2 %convolution_convert_fusion.5 = bf16[512,1792]{1,0:T(8,128)(2,1)} fusion(bf16[512,2048]{1,0:T(8,128)(2,1)S(1)} %copy-done, bf16[2048,1792]{1,0:T(8,128)(2,1)} %param.17), kind=kOutput, calls=%fused_computation.11 | convolution fusion | flops 3759013888 | bytes 11272192 | tf_op jit(solution)/shard_map/dot_general | solution.py:23
  25.2 24.4 %reduce-scatter.6.cloned.1.call-done = bf16[128,1792]{1,0:T(8,128)(2,1)} async-done(((bf16[512,1792]{1,0:T(8,128)(2,1)}), bf16[128,1792]{1,0:T(8,128)(2,1)}) %reduce-scatter.6.cloned.1.call-update) | async-done | bytes 458768 | tf_op jit(solution)/shard_map/reduce_scatter | solution.py:29
  49.6 33.1 %reduce-scatter.4.cloned.1.call-done = bf16[128,1792]{1,0:T(8,128)(2,1)} async-done(((bf16[512,1792]{1,0:T(8,128)(2,1)}), bf16[128,1792]{1,0:T(8,128)(2,1)}) %reduce-scatter.4.cloned.1.call-update) | async-done | bytes 458768 | tf_op jit(solution)/shard_map/reduce_scatter | solution.py:26
  85.0 21.2 %all-gather.4.cloned.1.call-done = bf16[512,1792]{1,0:T(8,128)(2,1)} async-done(((bf16[128,1792]{1,0:T(8,128)(2,1)}), bf16[512,1792]{1,0:T(8,128)(2,1)}) %all-gather.4.cloned.1.call-update) | async-done | bytes 1835024 | tf_op jit(solution)/shard_map/all_gather | solution.py:35
  106.3 8.9 %convolution_convert_fusion.3 = bf16[512,2048]{1,0:T(8,128)(2,1)} fusion(bf16[512,1792]{1,0:T(8,128)(2,1)} %all-gather.4.cloned.1.call-done, bf16[1792,2048]{1,0:T(8,128)(2,1)} %param.19), kind=kOutput, calls=%fused_computation.9 | convolution fusion | flops 3759144960 | bytes 11272192 | tf_op jit(solution)/shard_map/dot_general | solution.py:34
  118.5 4.6 fusion.15
  127.7 9.4 %copy.31 = bf16[512,8,4,256]{3,1,2,0:T(8,128)(2,1)} copy(bf16[512,8,4,256]{3,2,1,0:T(4,128)(2,1)} %bitcast.65) | data formatting | bytes 16777216
  137.2 46.3 %reduce-scatter.8.cloned.1.call-done = bf16[512,256]{1,0:T(8,128)(2,1)} async-done(((bf16[512,2048]{1,0:T(8,128)(2,1)}), bf16[512,256]{1,0:T(8,128)(2,1)}) %reduce-scatter.8.cloned.1.call-update) | async-done | bytes 262160 | tf_op jit(solution)/shard_map/reduce_scatter | solution.py:40
  187.6 76.9 %all-reduce.4.cloned.1.call-done = bf16[128,4096]{1,0:T(8,128)(2,1)} async-done(((bf16[128,4096]{1,0:T(8,128)(2,1)}), bf16[128,4096]{1,0:T(8,128)(2,1)}) %all-reduce.4.cloned.1.call-update) | async-done | bytes 1048592 | tf_op jit(solution)/shard_map/psum | solution.py:57
  267.0 5.4 %fusion.5 = bf16[128,1024]{1,0:T(8,128)(2,1)} fusion(f32[128,1024]{1,0:T(8,128)S(1)} %bitcast.67, bf16[128,4096]{1,0:T(8,128)(2,1)S(1)} %fusion.2, bf16[4096,1024]{1,0:T(8,128)(2,1)} %bitcast.57), kind=kOutput, calls=%fused_computation.21 | convolution fusion | flops 1074135040 | bytes 10223616 | tf_op jit(solution)/shard_map/dot_general | solution.py:63
  272.4 7.3 %convolution_convert_fusion = bf16[128,4096]{1,0:T(8,128)(2,1)} fusion(bf16[128,1024]{1,0:T(8,128)(2,1)} %fusion.5, bf16[4096,1024]{1,0:T(8,128)(2,1)} %bitcast.58), kind=kOutput, calls=%fused_computation.2 | convolution fusion | flops 1074266112 | bytes 9699328 | tf_op jit(solution)/shard_map/dot_general | solution.py:66
  280.7 76.7 %all-reduce.6.cloned.1.call-done = bf16[128,4096]{1,0:T(8,128)(2,1)} async-done(((bf16[128,4096]{1,0:T(8,128)(2,1)}), bf16[128,4096]{1,0:T(8,128)(2,1)}) %all-reduce.6.cloned.1.call-update) | async-done | bytes 1048592 | tf_op jit(solution)/shard_map/psum | solution.py:65
  357.5 6.0 %multiply_convert_fusion.2 = (bf16[128,896]{1,0:T(8,128)(2,1)S(1)}, bf16[128,896]{1,0:T(8,128)(2,1)S(1)}) fusion(f32[128,896]{1,0:T(8,128)} %copy-done.3, f32[128,896]{1,0:T(8,128)} %get-tuple-element.29, bf16[128,4096]{1,0:T(8,128)(2,1)} %all-reduce.6.cloned.1.call-done, bf16[896,4096]{1,0:T(8,128)(2,1)} %param.14), kind=kOutput, calls=%fused_computation.35 | convolution fusion | flops 941015040 | bytes 9764864 | tf_op jit(solution)/shard_map/dot_general | solution.py:70
  363.5 5.9 %fusion.16 = f32[128,4096]{1,0:T(8,128)S(1)} fusion(bf16[128,896]{1,0:T(8,128)(2,1)S(1)} %get-tuple-element.26, bf16[4096,896]{1,0:T(8,128)(2,1)} %param.12), kind=kOutput, calls=%fused_computation.47 | convolution fusion | flops 939524096 | bytes 9666560 | tf_op jit(solution)/shard_map/dot_general | solution.py:73
  369.4 6.6 %fusion = bf16[128,4096]{1,0:T(8,128)(2,1)} fusion(f32[128,4096]{1,0:T(8,128)S(1)} %fusion.16, bf16[128,896]{1,0:T(8,128)(2,1)S(1)} %get-tuple-element.27, bf16[4096,896]{1,0:T(8,128)(2,1)} %param.13), kind=kOutput, calls=%fused_computation.1 | convolution fusion | flops 940572672 | bytes 10715136 | tf_op jit(solution)/shard_map/dot_general | solution.py:73
  379.0 4.4 all-to-all-start.3
  384.5 13.5 %all-to-all-done.3 = bf16[128,4,1024]{2,0,1:T(8,128)(2,1)} async-done(((bf16[128,4,1024]{2,0,1:T(8,128)(2,1)}), bf16[128,4,1024]{2,0,1:T(8,128)(2,1)}, u32[]{:S(2)}, u32[]{:S(2)}) %all-to-all-start.3) | async-done | bytes 1048608 | tf_op jit(solution)/shard_map/all_to_all | solution.py:86
  397.9 4.3 all-to-all-start.2
  403.2 19.6 %all_gather.14 = bf16[512,896]{1,0:T(8,128)(2,1)} all-gather(bf16[128,896]{1,0:T(8,128)(2,1)S(1)} %get-tuple-element.28), channel_id=1, replica_groups=mesh['grp'=2,'wid'=4,'hid'=4] {'wid'}, dimensions={0}, use_global_device_ids=true | all-gather | bytes 1146880 | tf_op jit(solution)/shard_map/all_gather | solution.py:90
  422.8 4.2 convolution_convert_fusion.6
  427.1 4.2 copy.26
  438.7 19.5 %all-reduce.8.cloned.1.call-done = bf16[128,4096]{1,0:T(8,128)(2,1)} async-done(((bf16[128,4096]{1,0:T(8,128)(2,1)}), bf16[128,4096]{1,0:T(8,128)(2,1)}) %all-reduce.8.cloned.1.call-update) | async-done | bytes 1048592 | tf_op jit(solution)/shard_map/psum | solution.py:78
  461.7 18.9 %all-gather.6.cloned.1.call-done = bf16[512,1792]{1,0:T(8,128)(2,1)} async-done(((bf16[128,1792]{1,0:T(8,128)(2,1)}), bf16[512,1792]{1,0:T(8,128)(2,1)}) %all-gather.6.cloned.1.call-update) | async-done | bytes 1835024 | tf_op jit(solution)/shard_map/all_gather | solution.py:91
  (71 shorter events, 41.6 us)
Async XLA Ops:
  7.2 1.6 copy-start
  7.2 42.4 %reduce-scatter.6.cloned.1.call-start = ((), (), s32[]{:S(2)}) async-start(), calls=%async_computation.9 | async-start | bytes 2293760 | tf_op jit(solution)/shard_map/reduce_scatter | solution.py:29
  16.9 65.8 %reduce-scatter.4.cloned.1.call-start = ((), (), s32[]{:S(2)}) async-start(), calls=%async_computation.8 | async-start | bytes 2293760 | tf_op jit(solution)/shard_map/reduce_scatter | solution.py:26
  25.2 81.1 %all-gather.4.cloned.1.call-start = ((), (), s32[]{:S(2)}) async-start(), calls=%async_computation.10 | async-start | bytes 2293760 | tf_op jit(solution)/shard_map/all_gather | solution.py:35
  85.0 98.5 %reduce-scatter.8.cloned.1.call-start = ((), (), s32[]{:S(2)}) async-start(), calls=%async_computation.11 | async-start | bytes 2359296 | tf_op jit(solution)/shard_map/reduce_scatter | solution.py:40
  115.2 149.2 %all-reduce.4.cloned.1.call-start = ((), (), s32[]{:S(2)}) async-start(), calls=%async_computation.7 | async-start | bytes 2097152 | tf_op jit(solution)/shard_map/psum | solution.py:57
  116.7 6.4 %slice-start = ((s8[7340032]{0:T(1024)(128)(4,1)}), s8[4194304]{0:T(1024)(128)(4,1)S(1)}, s32[]{:S(2)}) async-start(s8[7340032]{0:T(1024)(128)(4,1)} %bitcast.59), calls=%async_computation.16 | async-start | bytes 8388608
  118.5 4.6 slice-start.1
  118.5 6.8 %slice-start.2 = ((s8[7340032]{0:T(1024)(128)(4,1)}), s8[4194304]{0:T(1024)(128)(4,1)S(1)}, s32[]{:S(2)}) async-start(s8[7340032]{0:T(1024)(128)(4,1)} %bitcast.62), calls=%async_computation.18 | async-start | bytes 8388608
  123.1 2.1 copy-start.3
  123.1 2.3 slice-start.3
  183.5 82.4 %all-to-all-start.1 = ((bf16[4,128,256]{2,1,0:T(8,128)(2,1)}), bf16[4,128,256]{2,1,0:T(8,128)(2,1)}, u32[]{:S(2)}, u32[]{:S(2)}) async-start(bf16[4,128,256]{2,1,0:T(8,128)(2,1)} %bitcast.71), calls=%async_computation.4 | async-start | bytes 524288 | tf_op jit(solution)/shard_map/all_to_all | solution.py:46
  187.6 169.9 %all-reduce.6.cloned.1.call-start = ((), (), s32[]{:S(2)}) async-start(), calls=%async_computation.12 | async-start | bytes 2097152 | tf_op jit(solution)/shard_map/psum | solution.py:65
  279.7 143.1 %all-gather.8.cloned.1.call-start = ((), (), s32[]{:S(2)}) async-start(), calls=%async_computation.14 | async-start | bytes 1310720 | tf_op jit(solution)/shard_map/all_gather | solution.py:92
  280.5 177.7 %all-reduce.8.cloned.1.call-start = ((), (), s32[]{:S(2)}) async-start(), calls=%async_computation.15 | async-start | bytes 2097152 | tf_op jit(solution)/shard_map/psum | solution.py:78
  363.5 5.9 %copy-start.6 = (bf16[128,896]{1,0:T(8,128)(2,1)}, bf16[128,896]{1,0:T(8,128)(2,1)S(1)}, u32[]{:S(2)}) copy-start(bf16[128,896]{1,0:T(8,128)(2,1)S(1)} %get-tuple-element.26) | copy-start | bytes 688132
  363.5 5.9 %copy-start.7 = (bf16[128,896]{1,0:T(8,128)(2,1)}, bf16[128,896]{1,0:T(8,128)(2,1)S(1)}, u32[]{:S(2)}) copy-start(bf16[128,896]{1,0:T(8,128)(2,1)S(1)} %get-tuple-element.27) | copy-start | bytes 688132
  376.0 104.6 %all-gather.6.cloned.1.call-start = ((), (), s32[]{:S(2)}) async-start(), calls=%async_computation.13 | async-start | bytes 2293760 | tf_op jit(solution)/shard_map/all_gather | solution.py:91
  379.0 4.4 copy-start.4
  379.0 18.9 %all-to-all-start.3 = ((bf16[128,4,1024]{2,0,1:T(8,128)(2,1)}), bf16[128,4,1024]{2,0,1:T(8,128)(2,1)}, u32[]{:S(2)}, u32[]{:S(2)}) async-start(bf16[128,4,1024]{2,0,1:T(8,128)(2,1)} %bitcast.66), calls=%async_computation.6 | async-start | bytes 2097152 | tf_op jit(solution)/shard_map/all_to_all | solution.py:86
  397.9 33.4 %all-to-all-start.2 = ((bf16[128,4,1024]{2,0,1:T(8,128)(2,1)}), bf16[128,4,1024]{2,0,1:T(8,128)(2,1)}, u32[]{:S(2)}, u32[]{:S(2)}) async-start(bf16[128,4,1024]{2,0,1:T(8,128)(2,1)} %bitcast.55), calls=%async_computation.5 | async-start | bytes 2097152 | tf_op jit(solution)/shard_map/all_to_all | solution.py:87
  431.3 30.4 %all-to-all-start = ((bf16[128,4,1024]{2,0,1:T(8,128)(2,1)}), bf16[128,4,1024]{2,0,1:T(8,128)(2,1)S(1)}, u32[]{:S(2)}, u32[]{:S(2)}) async-start(bf16[128,4,1024]{2,0,1:T(8,128)(2,1)} %bitcast.56), calls=%async_computation | async-start | bytes 2097152 | tf_op jit(solution)/shard_map/all_to_all | solution.py:85
  461.7 18.9 %copy-start.5 = (bf16[128,4,1024]{2,0,1:T(8,128)(2,1)}, bf16[128,4,1024]{2,0,1:T(8,128)(2,1)S(1)}, u32[]{:S(2)}) copy-start(bf16[128,4,1024]{2,0,1:T(8,128)(2,1)S(1)} %all-to-all-done) | copy-start | bytes 3145732
  480.6 6.2 %copy-start.1 = (bf16[512,2048]{1,0:T(8,128)(2,1)S(1)}, bf16[512,2048]{1,0:T(8,128)(2,1)}, u32[]{:S(2)}) copy-start(bf16[512,2048]{1,0:T(8,128)(2,1)} %param.16) | copy-start | bytes 6291460
  (2 other events, 2.7 us)
Sparse Core Ops, SparseCore 0:
  17.1 32.5 reduce-scatter.5
  52.9 29.8 reduce-scatter.3
  85.1 21.1 all-gather.3
  115.3 68.1 reduce-scatter.7
  187.4 76.9 all-reduce.3
  279.9 77.5 all-reduce.5
  359.6 16.3 all-gather.7
  380.0 78.1 all-reduce.7
  459.8 20.7 all-gather.5
where the time goes:
time: 494 us; the launch traced here: 493 us
  waiting for transfers between devices  331 us (67%)
  matrix products  77.6 us (16%)
  local copies, waits for them, and re-layouts  21.8 us (4%)
  blocking collectives  19.6 us (4%)
  starting transfers between devices  17 us (3%)
  between operations  14.1 us (3%)
  other arithmetic  12 us (2%)
    psum x1, waiting for transfers between devices, shards(): lax.psum(jnp.dot(hidden, down_weight, preferred_element_type=f32).astype(...  76.9 us
    psum x1, waiting for transfers between devices, shards(): lax.psum(jnp.dot(feature_error, proj_local.T, preferred_element_type=f32)...  76.7 us
    reduce_scatter x1, waiting for transfers between devices, shards(): lax.psum_scatter(feature_part.astype(jnp.bfloat16), ('grp', 'hid'), scatt...  46.3 us
    reduce_scatter x1, waiting for transfers between devices, shards(): lax.psum_scatter(gate_part.astype(jnp.bfloat16), 'wid', scatter_dimension...  33.1 us
    reduce_scatter x1, waiting for transfers between devices, shards(): lax.psum_scatter(up_part.astype(jnp.bfloat16), 'wid', scatter_dimension=0...  24.4 us
    all_gather x1, waiting for transfers between devices, shards(): lax.all_gather(teacher_hidden, 'wid', axis=0, tiled=True)  21.2 us
    all_gather x1, blocking collectives, shards(): lax.all_gather(hidden, 'wid', axis=0, tiled=True)  19.6 us
    psum x1, waiting for transfers between devices, shards(): lax.psum(normed_grad.astype(jnp.bfloat16), ('grp', 'hid'))  19.5 us
  transfers between devices with their start and end apart: 13, of which 9 were waited for; matrix products, arithmetic and copies ran while one was open for 14% of the time, Pallas kernels for 0%

commit v1 on v0

v1 whole, which is shorter than its diff:
```python
import math

import jax
import jax.numpy as jnp
from jax import lax
from jax.sharding import PartitionSpec as P

F32 = jnp.float32
BF16 = jnp.bfloat16
CORES = 2


def dot(a, b):
    return jnp.dot(a, b, preferred_element_type=F32)


def shift(x, axis, step):
    size = lax.axis_size(axis)
    return lax.ppermute(x, axis, [(i, (i + step) % size) for i in range(size)])


class Wid:
    def __init__(self):
        self.size = lax.axis_size("wid")
        self.cores = CORES if self.size % CORES == 0 else 1
        self.rows = self.size // self.cores
        self.index = lax.axis_index("wid")
        self.row = self.index // self.cores
        self.core = self.index % self.cores

    def at(self, drow, dcore):
        return ((self.row + drow) % self.rows) * self.cores + (self.core + dcore) % self.cores

    def send(self, x, drow, dcore):
        pairs = []
        for i in range(self.size):
            row, core = i // self.cores, i % self.cores
            pairs.append((i, ((row + drow) % self.rows) * self.cores + (core + dcore) % self.cores))
        return lax.ppermute(x, "wid", pairs)

    def gather(self, x):
        blocks = []
        for drow in range(self.rows):
            mine = x if drow == 0 else self.send(x, -drow, 0)
            blocks.append([mine] + [self.send(mine, 0, -dcore) for dcore in range(1, self.cores)])
        return blocks

    def swap(self, x):
        cols = x.shape[1] // self.size
        blocks = []
        for drow in range(self.rows):
            group = []
            for dcore in range(self.cores):
                block = lax.dynamic_slice_in_dim(x, self.at(-drow, -dcore) * cols, cols, 1)
                group.append(block if drow + dcore == 0 else self.send(block, -drow, -dcore))
            blocks.append(group)
        return blocks


def flat(blocks):
    return [b for group in blocks for b in group]


def scatter_sum(x):
    ngrp, nhid = lax.axis_size("grp"), lax.axis_size("hid")
    g, h = lax.axis_index("grp"), lax.axis_index("hid")
    cols = x.shape[1] // (ngrp * nhid)

    def block(dg, dh):
        return lax.dynamic_slice_in_dim(x, (((g + dg) % ngrp) * nhid + (h + dh) % nhid) * cols, cols, 1)

    total = None
    for dh in list(range(1, nhid)) + [0]:
        got = [shift(block(dg, dh), "grp", dg) for dg in range(1, ngrp)]
        part = block(0, dh).astype(F32)
        for r in got:
            part = part + r.astype(F32)
        if dh == 0:
            total = part if total is None else total + part
        else:
            r = shift(part.astype(BF16), "hid", dh).astype(F32)
            total = r if total is None else total + r
    return total


def gather_cols(x):
    ngrp, nhid = lax.axis_size("grp"), lax.axis_size("hid")
    g, h = lax.axis_index("grp"), lax.axis_index("hid")
    cols = x.shape[1]
    out = jnp.zeros((x.shape[0], cols * ngrp * nhid), x.dtype)
    for dh in range(nhid):
        mine = x if dh == 0 else shift(x, "hid", dh)
        for dg in range(ngrp):
            piece = mine if dg == 0 else shift(mine, "grp", dg)
            place = ((g - dg) % ngrp) * nhid + (h - dh) % nhid
            out = lax.dynamic_update_slice_in_dim(out, piece, place * cols, 1)
    return out


def shards(
    student_in,
    norm_gain,
    gate_weight,
    up_weight,
    down_weight,
    projection,
    teacher_in,
    teacher_gate,
    teacher_up,
    teacher_down,
):
    wid = Wid()
    tokens = student_in.shape[0]
    width = student_in.shape[1]
    total_tokens = tokens * wid.size
    hidden_cols = gate_weight.shape[1]

    groups = []
    for dcore in range(wid.cores):
        groups.append(
            jnp.concatenate(
                [
                    lax.dynamic_slice_in_dim(teacher_in, wid.at(drow, dcore) * tokens, tokens, 0)
                    for drow in range(wid.rows)
                ],
                axis=0,
            )
        )
    units = teacher_gate.shape[1]
    chunks = 2 if units % 256 == 0 else 1
    size = units // chunks
    feature_parts = [None] * wid.rows
    for k in range(chunks):
        sums = []
        for weight in (teacher_gate, teacher_up):
            part = weight[:, k * size : (k + 1) * size]
            got = [
                wid.send(dot(groups[dcore], part).astype(BF16), 0, dcore)
                for dcore in range(1, wid.cores)
            ]
            own = dot(groups[0], part)
            for r in got:
                own = own + r.astype(F32)
            rows = own[:tokens]
            for drow in range(1, wid.rows):
                sent = own[drow * tokens : (drow + 1) * tokens].astype(BF16)
                rows = rows + wid.send(sent, drow, 0).astype(F32)
            sums.append(rows)
        gate_rows, up_rows = sums
        teacher_hidden = (gate_rows * jax.nn.sigmoid(gate_rows) * up_rows).astype(BF16)
        down = teacher_down[k * size : (k + 1) * size]
        for drow, group in enumerate(wid.gather(teacher_hidden)):
            part = dot(jnp.concatenate(group, axis=0), down)
            feature_parts[drow] = part if feature_parts[drow] is None else feature_parts[drow] + part

    inputs = student_in.astype(F32)
    inverse_rms = lax.rsqrt(jnp.mean(inputs * inputs, axis=-1, keepdims=True) + 1e-05)
    normed = (inputs * inverse_rms * norm_gain).astype(BF16)
    gate_sum = dot(normed, gate_weight)
    up_sum = dot(normed, up_weight)
    sigma = jax.nn.sigmoid(gate_sum)
    hidden = (gate_sum * sigma * up_sum).astype(BF16)
    branch = scatter_sum(dot(hidden, down_weight).astype(BF16)).astype(BF16)
    summed = (inputs + gather_cols(branch).astype(F32)).astype(BF16)
    proj_local = projection.reshape(width, -1)
    features = dot(summed, proj_local)

    share = projection.shape[2]
    target = jnp.zeros((tokens, wid.size * share), BF16)
    for drow in range(wid.rows):
        cols = scatter_sum(feature_parts[drow].astype(BF16)).astype(BF16)
        for dcore in range(wid.cores):
            block = cols[dcore * tokens : (dcore + 1) * tokens]
            if drow + dcore:
                block = wid.send(block, drow, dcore)
            target = lax.dynamic_update_slice_in_dim(target, block, wid.at(-drow, -dcore) * share, 1)

    feature_error = ((features - target.astype(F32)) / math.sqrt(total_tokens)).astype(BF16)
    feature_share = scatter_sum(dot(feature_error, proj_local.T).astype(BF16))
    branch_grad = gather_cols(feature_share.astype(BF16))
    hidden_grad = dot(branch_grad, down_weight.T)
    gate_grad = (hidden_grad * up_sum * sigma * (1.0 + gate_sum * (1.0 - sigma))).astype(BF16)
    up_grad = (hidden_grad * gate_sum * sigma).astype(BF16)
    moment = lax.psum(
        jnp.sum(
            gate_grad.astype(F32) * gate_sum + up_grad.astype(F32) * up_sum, axis=-1, keepdims=True
        ),
        ("grp", "hid"),
    )
    normed_grad = dot(gate_grad, gate_weight.T) + dot(up_grad, up_weight.T)
    normed_share = scatter_sum(normed_grad.astype(BF16))
    share_cols = normed_share.shape[1]
    offset = lax.axis_index(("grp", "hid")) * share_cols
    gain_share = lax.dynamic_slice_in_dim(norm_gain, offset, share_cols, 0)
    inputs_share = lax.dynamic_slice_in_dim(student_in, offset, share_cols, 1).astype(F32)
    input_grad = feature_share + inverse_rms * (
        normed_share * gain_share - inputs_share * inverse_rms * (moment / width)
    )

    def columns(x):
        return jnp.concatenate(flat(wid.swap(x)), axis=0)

    def everyone(x):
        return jnp.concatenate(flat(wid.gather(x)), axis=0)

    normed_cols = columns(normed)
    grad_proj = dot(columns(summed).T, everyone(feature_error)).astype(BF16)
    grad_proj = grad_proj.reshape(-1, wid.size, share)
    grad_down = dot(everyone(hidden).T, columns(branch_grad)).astype(BF16)
    grad_gate = dot(normed_cols.T, everyone(gate_grad)).astype(BF16)
    grad_up = dot(normed_cols.T, everyone(up_grad)).astype(BF16)
    return (grad_gate, grad_up, grad_down, grad_proj, input_grad)


def solution(mesh):
    in_specs = (
        P("wid", None),
        P(),
        P(None, ("grp", "hid")),
        P(None, ("grp", "hid")),
        P(("grp", "hid"), None),
        P(None, None, ("grp", "hid")),
        P(None, "wid"),
        P("wid", ("grp", "hid")),
        P("wid", ("grp", "hid")),
        P(("grp", "hid"), "wid"),
    )
    out_specs = (
        P("wid", ("grp", "hid")),
        P("wid", ("grp", "hid")),
        P(("grp", "hid"), "wid"),
        P("wid", None, ("grp", "hid")),
        P("wid", ("grp", "hid")),
    )
    return jax.shard_map(shards, mesh=mesh, in_specs=in_specs, out_specs=out_specs, check_vma=False)
```

time: 494 us -> 330 us (0.67)
  waiting for transfers between devices: 331 us -> 91.7 us
  starting transfers between devices: 17 us -> 92.5 us
  local copies, waits for them, and re-layouts: 21.8 us -> 35.5 us
  between operations: 14.1 us -> 1.91 us
    psum x3 -> x0, waiting for transfers between devices: 173 us -> none  [the longest x1 76.9 us: shards(): lax.psum(jnp.dot(hidden, down_weight, preferred_element_type=f32).astype(...]
    reduce_scatter x3 -> x0, waiting for transfers between devices: 104 us -> none  [the longest x1 46.3 us: shards(): lax.psum_scatter(feature_part.astype(jnp.bfloat16), ('grp', 'hid'), scatt...]
    ppermute x0 -> x87, starting transfers between devices: none -> 92.5 us  [the longest x49 74.4 us: shift(): return lax.ppermute(x, axis, [(i, (i + step) % size) for i in range(size)])]
    ppermute x0 -> x87, waiting for transfers between devices: none -> 91.7 us  [the longest x49 55.8 us: shift(): return lax.ppermute(x, axis, [(i, (i + step) % size) for i in range(size)])]
    all_gather x3 -> x0, waiting for transfers between devices: 40.2 us -> none  [the longest x1 21.2 us: shards(): lax.all_gather(teacher_hidden, 'wid', axis=0, tiled=True)]
    psum x0 -> x1, blocking collectives: none -> 19.8 us  [shards(): lax.psum(jnp.sum(gate_grad.astype(F32) * gate_sum + up_grad.astype(F32) *...]
    all_gather x1 -> x0, blocking collectives: 19.6 us -> none  [shards(): lax.all_gather(hidden, 'wid', axis=0, tiled=True)]
    all_to_all x4 -> x0, starting transfers between devices: 16.2 us -> none  [the longest x1 4.37 us: shards(): lax.all_to_all(summed, 'wid', split_axis=1, concat_axis=0, tiled=True)]
  transfers between devices with their start and end apart: 13 -> 87, of which waited for: 9 -> 33; matrix products, arithmetic and copies ran while one was open for 14% -> 30% of each run, Pallas kernels for 0% -> 0%
where the time goes in v1:
time: 330 us; the launch traced here: 326 us
  starting transfers between devices  92.5 us (28%)
  waiting for transfers between devices  91.7 us (28%)
  matrix products  74 us (22%)
  local copies, waits for them, and re-layouts  35.5 us (11%)
  blocking collectives  19.8 us (6%)
  other arithmetic  10.5 us (3%)
    ppermute x49, starting transfers between devices, shift(): return lax.ppermute(x, axis, [(i, (i + step) % size) for i in range(size)])  74.4 us
    dot_general x24, matrix products, dot(): return jnp.dot(a, b, preferred_element_type=F32)  74 us
    ppermute x49, waiting for transfers between devices, shift(): return lax.ppermute(x, axis, [(i, (i + step) % size) for i in range(size)])  55.8 us
    ppermute x38, waiting for transfers between devices, send(): return lax.ppermute(x, 'wid', pairs)  35.9 us
    psum x1, blocking collectives, shards(): lax.psum(jnp.sum(gate_grad.astype(F32) * gate_sum + up_grad.astype(F32) *...  19.8 us
    ppermute x38, starting transfers between devices, send(): return lax.ppermute(x, 'wid', pairs)  18.1 us
    unnamed x88, local copies, waits for them, and re-layouts  17.5 us
    dynamic_update_slice x14, local copies, waits for them, and re-layouts, gather_cols(): out = lax.dynamic_update_slice_in_dim(out, piece, place * cols, 1)  11.1 us
  transfers between devices with their start and end apart: 87, of which 33 were waited for; matrix products, arithmetic and copies ran while one was open for 30% of the time, Pallas kernels for 0%

profile of v1, /device:TPU:0, one launch (start us, length us, event | category | flops | bytes accessed | tf_op | source)
XLA Modules:
  0.0 326.0 jit_solution(16893259887663865968)
XLA Ops:
  3.4 4.5 %fusion.47 = bf16[256,896]{1,0:T(8,128)(2,1)} fusion(bf16[2048,1792]{1,0:T(8,128)(2,1)} %param.17, bf16[128,2048]{1,0:T(8,128)(2,1)S(1)} %get-tuple-element.19, bf16[128,2048]{1,0:T(8,128)(2,1)S(1)} %get-tuple-element.20), kind=kOutput, calls=%fused_computation.45 | convolution fusion | flops 941850624 | bytes 5177344 | tf_op jit(solution)/shard_map/dot_general | solution.py:14
  9.1 4.5 %fusion.133 = f32[128,896]{1,0:T(8,128)S(1)} fusion(bf16[128,4096]{1,0:T(8,128)(2,1)S(1)} %fusion.39, bf16[4096,896]{1,0:T(8,128)(2,1)} %param.12), kind=kOutput, calls=%fused_computation.217 | convolution fusion | flops 939524096 | bytes 8847360 | tf_op jit(solution)/shard_map/dot_general | solution.py:14
  40.7 4.4 %fusion.50 = bf16[256,896]{1,0:T(8,128)(2,1)} fusion(bf16[2048,1792]{1,0:T(8,128)(2,1)} %param.18, bf16[128,2048]{1,0:T(8,128)(2,1)} %copy-done.10, bf16[128,2048]{1,0:T(8,128)(2,1)} %copy-done.12), kind=kOutput, calls=%fused_computation.46 | convolution fusion | flops 941850624 | bytes 5177344 | tf_op jit(solution)/shard_map/dot_general | solution.py:14
  54.1 4.4 %fusion.44 = bf16[256,896]{1,0:T(8,128)(2,1)} fusion(bf16[2048,1792]{1,0:T(8,128)(2,1)} %param.18, bf16[128,2048]{1,0:T(8,128)(2,1)} %copy-done.10, bf16[128,2048]{1,0:T(8,128)(2,1)} %copy-done.12), kind=kOutput, calls=%fused_computation.44 | convolution fusion | flops 941850624 | bytes 5177344 | tf_op jit(solution)/shard_map/dot_general | solution.py:14
  58.5 9.5 %copy.16 = bf16[512,8,4,256]{3,1,2,0:T(8,128)(2,1)} copy(bf16[512,8,4,256]{3,2,1,0:T(4,128)(2,1)} %bitcast.32) | data formatting | bytes 16777216
  72.8 3.8 %convert_add_fusion.2 = f32[256,896]{1,0:T(8,128)S(1)} fusion(bf16[256,896]{1,0:T(8,128)(2,1)} %collective-permute-done.22, bf16[2048,1792]{1,0:T(8,128)(2,1)} %param.17, bf16[128,2048]{1,0:T(8,128)(2,1)} %get-tuple-element.18, bf16[128,2048]{1,0:T(8,128)(2,1)} %get-tuple-element.17), kind=kOutput, calls=%fused_computation.96 | convolution fusion | flops 942080000 | bytes 6094848 | tf_op jit(solution)/shard_map/dot_general | solution.py:14
  82.5 3.5 %convert_add_fusion.1 = f32[256,896]{1,0:T(8,128)S(1)} fusion(bf16[256,896]{1,0:T(8,128)(2,1)} %collective-permute-done.24, bf16[2048,1792]{1,0:T(8,128)(2,1)} %param.18, bf16[128,2048]{1,0:T(8,128)(2,1)S(1)} %copy-done.9, bf16[128,2048]{1,0:T(8,128)(2,1)S(1)} %copy-done.8), kind=kOutput, calls=%fused_computation.95 | convolution fusion | flops 942080000 | bytes 6094848 | tf_op jit(solution)/shard_map/dot_general | solution.py:14
  94.6 4.2 %collective-permute-done.25 = bf16[128,896]{1,0:T(8,128)(2,1)S(1)} collective-permute-done((bf16[128,896]{1,0:T(8,128)(2,1)S(1)}, bf16[128,896]{1,0:T(8,128)(2,1)S(1)}, u32[]{:S(2)}, u32[]{:S(2)}) %collective-permute-start.25) | collective-permute-done | bytes 229408 | tf_op jit(solution)/shard_map/ppermute | solution.py:39
  103.8 4.9 %collective-permute-done.20 = bf16[128,896]{1,0:T(8,128)(2,1)S(1)} collective-permute-done((bf16[128,896]{1,0:T(8,128)(2,1)S(1)}, bf16[128,896]{1,0:T(8,128)(2,1)S(1)}, u32[]{:S(2)}, u32[]{:S(2)}) %collective-permute-start.20) | collective-permute-done | bytes 229408 | tf_op jit(solution)/shard_map/ppermute | solution.py:39
  145.8 12.7 %collective-permute-start.44 = (bf16[256,256]{1,0:T(8,128)(2,1)S(1)}, bf16[256,256]{1,0:T(8,128)(2,1)S(1)}, u32[]{:S(2)}, u32[]{:S(2)}) collective-permute-start(bf16[256,256]{1,0:T(8,128)(2,1)S(1)} %get-tuple-element.48), channel_id=1, source_target_pairs={{0,3},{1,0},{2,1},{3,2},{4,7},{5,4},{6,5},{7,6},{8,11},{9,8},{10,9... | collective-permute-start | bytes 393224 | tf_op jit(solution)/shard_map/ppermute | solution.py:19
  161.6 4.4 %collective-permute-done.46 = bf16[128,256]{1,0:T(8,128)(2,1)S(1)} collective-permute-done((bf16[128,256]{1,0:T(8,128)(2,1)S(1)}, bf16[128,256]{1,0:T(8,128)(2,1)S(1)}, u32[]{:S(2)}, u32[]{:S(2)}) %collective-permute-start.46) | collective-permute-done | bytes 65568 | tf_op jit(solution)/shard_map/ppermute | solution.py:39
  168.0 3.8 %convolution_convert_fusion = bf16[128,4096]{1,0:T(8,128)(2,1)S(1)} fusion(bf16[128,1024]{1,0:T(8,128)(2,1)} %fusion.54, bf16[4096,1024]{1,0:T(8,128)(2,1)S(1)} %bitcast.25), kind=kOutput, calls=%fused_computation.2 | convolution fusion | flops 1074266112 | bytes 9699328 | tf_op jit(solution)/shard_map/dot_general | solution.py:14
  194.2 4.1 %collective-permute-done.51 = bf16[128,512]{1,0:T(8,128)(2,1)} collective-permute-done((bf16[128,512]{1,0:T(8,128)(2,1)}, bf16[128,512]{1,0:T(8,128)(2,1)}, u32[]{:S(2)}, u32[]{:S(2)}) %collective-permute-start.51) | collective-permute-done | bytes 131104 | tf_op jit(solution)/shard_map/ppermute | solution.py:19
  213.9 4.7 %collective-permute-done.76 = bf16[128,1024]{1,0:T(8,128)(2,1)S(1)} collective-permute-done((bf16[128,1024]{1,0:T(8,128)(2,1)S(1)}, bf16[128,1024]{1,0:T(8,128)(2,1)S(1)}, u32[]{:S(2)}, u32[]{:S(2)}) %collective-permute-start.76) | collective-permute-done | bytes 262176 | tf_op jit(solution)/shard_map/ppermute | solution.py:39
  222.0 3.7 %convolution_convert_fusion.2 = bf16[1024,1024]{0,1:T(8,128)(2,1)} fusion(bf16[128,1024]{1,0:T(8,128)(2,1)S(1)} %collective-permute-done.76, bf16[128,1024]{1,0:T(8,128)(2,1)S(1)} %collective-permute-done.75, bf16[128,1024]{1,0:T(8,128)(2,1)S(1)} %collective-permute-done.74, bf16[128,1024]{1,0:T(8,128)(2,1)S(1)} %get-tuple-element.28, ...), kind=kOutput, calls=%fused_computation.39 | convolution fusion | flops 1083179008 | bytes 4194304 | tf_op jit(solution)/shard_map/dot_general | solution.py:14
  225.7 4.4 %copy.15 = bf16[1024,4,256]{2,1,0:T(4,128)(2,1)} copy(bf16[1024,4,256]{0,2,1:T(8,128)(2,1)} %bitcast.33) | data formatting | bytes 4194304
  240.1 6.3 %add_reduce_fusion = (f32[128]{0:T(128)S(1)}, bf16[128,896]{1,0:T(8,128)(2,1)S(1)}, bf16[128,896]{1,0:T(8,128)(2,1)S(1)}) fusion(f32[128,896]{1,0:T(8,128)} %get-tuple-element.73, f32[128,896]{1,0:T(8,128)} %copy-done.7, bf16[128,4096]{1,0:T(8,128)(2,1)} %constant_dynamic-update-slice_fusion, bf16[896,4096]{1,0:T(8,128)(2,1)} %param.14), kind=kOutput, calls=%fused_computation.123 | convolution fusion | flops 941703040 | bytes 9765376 | tf_op jit(solution)/shard_map/dot_general | solution.py:14
  248.9 5.7 %fusion = bf16[128,4096]{1,0:T(8,128)(2,1)S(1)} fusion(f32[128,4096]{1,0:T(8,128)S(1)} %fusion.134, bf16[128,896]{1,0:T(8,128)(2,1)S(1)} %get-tuple-element.11, bf16[4096,896]{1,0:T(8,128)(2,1)} %param.13), kind=kOutput, calls=%fused_computation.1 | convolution fusion | flops 940572672 | bytes 10715136 | tf_op jit(solution)/shard_map/dot_general | solution.py:14
  257.4 19.8 %psum.7 = f32[128,1]{0,1:T(1,128)S(1)} all-reduce(f32[128,1]{0,1:T(1,128)S(1)} %bitcast.42), channel_id=1, replica_groups=mesh['grp'=2,'wid'=4,'hid'=4] {'grp','hid'}, use_global_device_ids=true, to_apply=%region_2.3 | all-reduce | flops 128 | bytes 1024 | tf_op jit(solution)/shard_map/psum | solution.py:184
  288.6 10.2 %collective-permute-done.66 = bf16[128,896]{1,0:T(8,128)(2,1)S(1)} collective-permute-done((bf16[128,896]{1,0:T(8,128)(2,1)S(1)}, bf16[128,896]{1,0:T(8,128)(2,1)S(1)}, u32[]{:S(2)}, u32[]{:S(2)}) %collective-permute-start.66) | collective-permute-done | bytes 229408 | tf_op jit(solution)/shard_map/ppermute | solution.py:39
  299.0 4.0 %collective-permute-start.85 = (bf16[128,512]{1,0:T(8,128)(2,1)S(1)}, bf16[128,512]{1,0:T(8,128)(2,1)S(1)}, u32[]{:S(2)}, u32[]{:S(2)}) collective-permute-start(bf16[128,512]{1,0:T(8,128)(2,1)S(1)} %get-tuple-element.22), channel_id=1, source_target_pairs={{0,3},{1,0},{2,1},{3,2},{4,7},{5,4},{6,5},{7,6},{8,11},{9,8},{10,9... | collective-permute-start | bytes 393224 | tf_op jit(solution)/shard_map/ppermute | solution.py:19
  303.0 3.6 %convolution_convert_fusion.3 = bf16[896,1024]{1,0:T(8,128)(2,1)} fusion(bf16[128,1024]{1,0:T(8,128)(2,1)S(1)} %collective-permute-done.73, bf16[128,1024]{1,0:T(8,128)(2,1)S(1)} %collective-permute-done.72, bf16[128,1024]{1,0:T(8,128)(2,1)S(1)} %collective-permute-done.71, bf16[128,1024]{1,0:T(8,128)(2,1)S(1)} %get-tuple-element.32, ...), kind=kOutput, calls=%fused_computation.40 | convolution fusion | flops 948305920 | bytes 3801088 | tf_op jit(solution)/shard_map/dot_general | solution.py:14
  307.1 4.7 %collective-permute-done.83 = bf16[128,512]{1,0:T(8,128)(2,1)S(1)} collective-permute-done((bf16[128,512]{1,0:T(8,128)(2,1)S(1)}, bf16[128,512]{1,0:T(8,128)(2,1)S(1)}, u32[]{:S(2)}, u32[]{:S(2)}) %collective-permute-start.83) | collective-permute-done | bytes 131104 | tf_op jit(solution)/shard_map/ppermute | solution.py:19
  315.0 3.7 %collective-permute-done.63 = bf16[128,896]{1,0:T(8,128)(2,1)S(1)} collective-permute-done((bf16[128,896]{1,0:T(8,128)(2,1)S(1)}, bf16[128,896]{1,0:T(8,128)(2,1)S(1)}, u32[]{:S(2)}, u32[]{:S(2)}) %collective-permute-start.63) | collective-permute-done | bytes 229408 | tf_op jit(solution)/shard_map/ppermute | solution.py:39
  (324 shorter events, 184.4 us)
Async XLA Ops:
  7.9 64.1 %collective-permute-start.22 = (bf16[256,896]{1,0:T(8,128)(2,1)}, bf16[256,896]{1,0:T(8,128)(2,1)}, u32[]{:S(2)}, u32[]{:S(2)}) collective-permute-start(bf16[256,896]{1,0:T(8,128)(2,1)} %fusion.47), channel_id=1, source_target_pairs={{0,4},{4,0},{8,12},{12,8},{1,5},{5,1},{9,13},{13,9},{2,6},{6,2},{1... | collective-permute-start | bytes 1376264 | tf_op jit(solution)/shard_map/ppermute | solution.py:39
  24.6 20.5 %collective-permute-start.9 = (bf16[128,512]{1,0:T(8,128)(2,1)}, bf16[128,512]{1,0:T(8,128)(2,1)S(1)}, u32[]{:S(2)}, u32[]{:S(2)}) collective-permute-start(bf16[128,512]{1,0:T(8,128)(2,1)} %get-tuple-element.65), channel_id=1, source_target_pairs={{0,16},{16,0},{1,17},{17,1},{2,18},{18,2},{3,19},{19,3},{4,20},{20... | collective-permute-start | bytes 393224 | tf_op jit(solution)/shard_map/ppermute | solution.py:19
  45.1 35.9 %collective-permute-start.24 = (bf16[256,896]{1,0:T(8,128)(2,1)}, bf16[256,896]{1,0:T(8,128)(2,1)}, u32[]{:S(2)}, u32[]{:S(2)}) collective-permute-start(bf16[256,896]{1,0:T(8,128)(2,1)} %fusion.50), channel_id=1, source_target_pairs={{0,4},{4,0},{8,12},{12,8},{1,5},{5,1},{9,13},{13,9},{2,6},{6,2},{1... | collective-permute-start | bytes 1376264 | tf_op jit(solution)/shard_map/ppermute | solution.py:39
  45.1 41.0 %collective-permute-start.17 = (bf16[256,896]{1,0:T(8,128)(2,1)}, bf16[256,896]{1,0:T(8,128)(2,1)}, u32[]{:S(2)}, u32[]{:S(2)}) collective-permute-start(bf16[256,896]{1,0:T(8,128)(2,1)} %fusion.41), channel_id=1, source_target_pairs={{0,4},{4,0},{8,12},{12,8},{1,5},{5,1},{9,13},{13,9},{2,6},{6,2},{1... | collective-permute-start | bytes 1376264 | tf_op jit(solution)/shard_map/ppermute | solution.py:39
  49.5 18.4 %collective-permute-start.10 = (bf16[128,512]{1,0:T(8,128)(2,1)S(1)}, bf16[128,512]{1,0:T(8,128)(2,1)}, u32[]{:S(2)}, u32[]{:S(2)}) collective-permute-start(bf16[128,512]{1,0:T(8,128)(2,1)S(1)} %get-tuple-element.16), channel_id=1, source_target_pairs={{0,16},{16,0},{1,17},{17,1},{2,18},{18,2},{3,19},{19,3},{4,20},{20... | collective-permute-start | bytes 393224 | tf_op jit(solution)/shard_map/ppermute | solution.py:19
  51.1 17.8 %collective-permute-start.11 = (bf16[128,512]{1,0:T(8,128)(2,1)S(1)}, bf16[128,512]{1,0:T(8,128)(2,1)}, u32[]{:S(2)}, u32[]{:S(2)}) collective-permute-start(bf16[128,512]{1,0:T(8,128)(2,1)S(1)} %get-tuple-element.16), channel_id=1, source_target_pairs={{0,1},{1,2},{2,3},{3,0},{4,5},{5,6},{6,7},{7,4},{8,9},{9,10},{10,1... | collective-permute-start | bytes 393224 | tf_op jit(solution)/shard_map/ppermute | solution.py:19
  68.0 22.2 %collective-permute-start.19 = (bf16[256,896]{1,0:T(8,128)(2,1)}, bf16[256,896]{1,0:T(8,128)(2,1)S(1)}, u32[]{:S(2)}, u32[]{:S(2)}) collective-permute-start(bf16[256,896]{1,0:T(8,128)(2,1)} %fusion.44), channel_id=1, source_target_pairs={{0,4},{4,0},{8,12},{12,8},{1,5},{5,1},{9,13},{13,9},{2,6},{6,2},{1... | collective-permute-start | bytes 1376264 | tf_op jit(solution)/shard_map/ppermute | solution.py:39
  99.0 18.1 %collective-permute-start.37 = (bf16[128,896]{1,0:T(8,128)(2,1)S(1)}, bf16[128,896]{1,0:T(8,128)(2,1)S(1)}, u32[]{:S(2)}, u32[]{:S(2)}) collective-permute-start(bf16[128,896]{1,0:T(8,128)(2,1)S(1)} %fusion.98), channel_id=1, source_target_pairs={{0,8},{4,12},{8,0},{12,4},{1,9},{5,13},{9,1},{13,5},{2,10},{6,14},... | collective-permute-start | bytes 688136 | tf_op jit(solution)/shard_map/ppermute | solution.py:39
  117.1 17.1 %collective-permute-start.33 = (bf16[256,256]{1,0:T(8,128)(2,1)S(1)}, bf16[256,256]{1,0:T(8,128)(2,1)S(1)}, u32[]{:S(2)}, u32[]{:S(2)}) collective-permute-start(bf16[256,256]{1,0:T(8,128)(2,1)S(1)} %get-tuple-element.58), channel_id=1, source_target_pairs={{0,16},{16,0},{1,17},{17,1},{2,18},{18,2},{3,19},{19,3},{4,20},{20... | collective-permute-start | bytes 393224 | tf_op jit(solution)/shard_map/ppermute | solution.py:19
  138.3 20.3 %collective-permute-start.45 = (bf16[256,256]{1,0:T(8,128)(2,1)S(1)}, bf16[256,256]{1,0:T(8,128)(2,1)S(1)}, u32[]{:S(2)}, u32[]{:S(2)}) collective-permute-start(bf16[256,256]{1,0:T(8,128)(2,1)S(1)} %get-tuple-element.51), channel_id=1, source_target_pairs={{0,16},{16,0},{1,17},{17,1},{2,18},{18,2},{3,19},{19,3},{4,20},{20... | collective-permute-start | bytes 393224 | tf_op jit(solution)/shard_map/ppermute | solution.py:19
  145.8 15.5 %collective-permute-start.44 = (bf16[256,256]{1,0:T(8,128)(2,1)S(1)}, bf16[256,256]{1,0:T(8,128)(2,1)S(1)}, u32[]{:S(2)}, u32[]{:S(2)}) collective-permute-start(bf16[256,256]{1,0:T(8,128)(2,1)S(1)} %get-tuple-element.48), channel_id=1, source_target_pairs={{0,3},{1,0},{2,1},{3,2},{4,7},{5,4},{6,5},{7,6},{8,11},{9,8},{10,9... | collective-permute-start | bytes 393224 | tf_op jit(solution)/shard_map/ppermute | solution.py:19
  175.8 15.3 %collective-permute-start.54 = (bf16[128,512]{1,0:T(8,128)(2,1)}, bf16[128,512]{1,0:T(8,128)(2,1)S(1)}, u32[]{:S(2)}, u32[]{:S(2)}) collective-permute-start(bf16[128,512]{1,0:T(8,128)(2,1)} %get-tuple-element.44), channel_id=1, source_target_pairs={{0,16},{16,0},{1,17},{17,1},{2,18},{18,2},{3,19},{19,3},{4,20},{20... | collective-permute-start | bytes 393224 | tf_op jit(solution)/shard_map/ppermute | solution.py:19
  212.8 17.3 %collective-permute-start.69 = (bf16[128,896]{1,0:T(8,128)(2,1)S(1)}, bf16[128,896]{1,0:T(8,128)(2,1)}, u32[]{:S(2)}, u32[]{:S(2)}) collective-permute-start(bf16[128,896]{1,0:T(8,128)(2,1)S(1)} %get-tuple-element.72), channel_id=1, source_target_pairs={{0,8},{4,12},{8,0},{12,4},{1,9},{5,13},{9,1},{13,5},{2,10},{6,14},... | collective-permute-start | bytes 688136 | tf_op jit(solution)/shard_map/ppermute | solution.py:39
  213.9 63.4 %collective-permute-start.68 = (bf16[128,896]{1,0:T(8,128)(2,1)S(1)}, bf16[128,896]{1,0:T(8,128)(2,1)}, u32[]{:S(2)}, u32[]{:S(2)}) collective-permute-start(bf16[128,896]{1,0:T(8,128)(2,1)S(1)} %get-tuple-element.72), channel_id=1, source_target_pairs={{0,4},{4,0},{8,12},{12,8},{1,5},{5,1},{9,13},{13,9},{2,6},{6,2},{1... | collective-permute-start | bytes 688136 | tf_op jit(solution)/shard_map/ppermute | solution.py:39
  230.1 49.0 %collective-permute-start = (bf16[128,1024]{1,0:T(8,128)(2,1)}, bf16[128,1024]{1,0:T(8,128)(2,1)}, u32[]{:S(2)}, u32[]{:S(2)}) collective-permute-start(bf16[128,1024]{1,0:T(8,128)(2,1)} %get-tuple-element.39), channel_id=1, source_target_pairs={{0,4},{4,0},{8,12},{12,8},{1,5},{5,1},{9,13},{13,9},{2,6},{6,2},{1... | collective-permute-start | bytes 786440 | tf_op jit(solution)/shard_map/ppermute | solution.py:39
  230.1 49.0 %collective-permute-start.70 = (bf16[128,896]{1,0:T(8,128)(2,1)}, bf16[128,896]{1,0:T(8,128)(2,1)}, u32[]{:S(2)}, u32[]{:S(2)}) collective-permute-start(bf16[128,896]{1,0:T(8,128)(2,1)} %collective-permute-done.69), channel_id=1, source_target_pairs={{0,4},{4,0},{8,12},{12,8},{1,5},{5,1},{9,13},{13,9},{2,6},{6,2},{1... | collective-permute-start | bytes 688136 | tf_op jit(solution)/shard_map/ppermute | solution.py:39
  255.4 24.3 %collective-permute-start.80 = (bf16[128,512]{1,0:T(8,128)(2,1)}, bf16[128,512]{1,0:T(8,128)(2,1)}, u32[]{:S(2)}, u32[]{:S(2)}) collective-permute-start(bf16[128,512]{1,0:T(8,128)(2,1)} %get-tuple-element.24), channel_id=1, source_target_pairs={{0,16},{16,0},{1,17},{17,1},{2,18},{18,2},{3,19},{19,3},{4,20},{20... | collective-permute-start | bytes 393224 | tf_op jit(solution)/shard_map/ppermute | solution.py:19
  256.5 24.5 %collective-permute-start.82 = (bf16[128,512]{1,0:T(8,128)(2,1)}, bf16[128,512]{1,0:T(8,128)(2,1)}, u32[]{:S(2)}, u32[]{:S(2)}) collective-permute-start(bf16[128,512]{1,0:T(8,128)(2,1)} %get-tuple-element.27), channel_id=1, source_target_pairs={{0,16},{16,0},{1,17},{17,1},{2,18},{18,2},{3,19},{19,3},{4,20},{20... | collective-permute-start | bytes 393224 | tf_op jit(solution)/shard_map/ppermute | solution.py:19
  279.1 19.7 %collective-permute-start.71 = (bf16[128,1024]{1,0:T(8,128)(2,1)S(1)}, bf16[128,1024]{1,0:T(8,128)(2,1)S(1)}, u32[]{:S(2)}, u32[]{:S(2)}) collective-permute-start(bf16[128,1024]{1,0:T(8,128)(2,1)S(1)} %get-tuple-element.35), channel_id=1, source_target_pairs={{0,4},{4,0},{8,12},{12,8},{1,5},{5,1},{9,13},{13,9},{2,6},{6,2},{1... | collective-permute-start | bytes 786440 | tf_op jit(solution)/shard_map/ppermute | solution.py:39
  279.1 19.8 %collective-permute-start.72 = (bf16[128,1024]{1,0:T(8,128)(2,1)S(1)}, bf16[128,1024]{1,0:T(8,128)(2,1)S(1)}, u32[]{:S(2)}, u32[]{:S(2)}) collective-permute-start(bf16[128,1024]{1,0:T(8,128)(2,1)S(1)} %get-tuple-element.34), channel_id=1, source_target_pairs={{0,8},{4,12},{8,0},{12,4},{1,9},{5,13},{9,1},{13,5},{2,10},{6,14},... | collective-permute-start | bytes 786440 | tf_op jit(solution)/shard_map/ppermute | solution.py:39
  279.7 19.3 %collective-permute-start.73 = (bf16[128,1024]{1,0:T(8,128)(2,1)S(1)}, bf16[128,1024]{1,0:T(8,128)(2,1)S(1)}, u32[]{:S(2)}, u32[]{:S(2)}) collective-permute-start(bf16[128,1024]{1,0:T(8,128)(2,1)S(1)} %get-tuple-element.33), channel_id=1, source_target_pairs={{0,12},{4,8},{8,4},{12,0},{1,13},{5,9},{9,5},{13,1},{2,14},{6,10},... | collective-permute-start | bytes 786440 | tf_op jit(solution)/shard_map/ppermute | solution.py:39
  281.0 17.8 %collective-permute-start.66 = (bf16[128,896]{1,0:T(8,128)(2,1)S(1)}, bf16[128,896]{1,0:T(8,128)(2,1)S(1)}, u32[]{:S(2)}, u32[]{:S(2)}) collective-permute-start(bf16[128,896]{1,0:T(8,128)(2,1)S(1)} %copy-done.20), channel_id=1, source_target_pairs={{0,8},{4,12},{8,0},{12,4},{1,9},{5,13},{9,1},{13,5},{2,10},{6,14},... | collective-permute-start | bytes 688136 | tf_op jit(solution)/shard_map/ppermute | solution.py:39
  288.1 26.5 %collective-permute-start.1 = (bf16[128,1024]{1,0:T(8,128)(2,1)S(1)}, bf16[128,1024]{1,0:T(8,128)(2,1)S(1)}, u32[]{:S(2)}, u32[]{:S(2)}) collective-permute-start(bf16[128,1024]{1,0:T(8,128)(2,1)S(1)} %copy-done.16), channel_id=1, source_target_pairs={{0,8},{4,12},{8,0},{12,4},{1,9},{5,13},{9,1},{13,5},{2,10},{6,14},... | collective-permute-start | bytes 786440 | tf_op jit(solution)/shard_map/ppermute | solution.py:39
  298.8 19.9 %collective-permute-start.2 = (bf16[128,1024]{1,0:T(8,128)(2,1)S(1)}, bf16[128,1024]{1,0:T(8,128)(2,1)S(1)}, u32[]{:S(2)}, u32[]{:S(2)}) collective-permute-start(bf16[128,1024]{1,0:T(8,128)(2,1)S(1)} %copy-done.15), channel_id=1, source_target_pairs={{0,12},{4,8},{8,4},{12,0},{1,13},{5,9},{9,5},{13,1},{2,14},{6,10},... | collective-permute-start | bytes 786440 | tf_op jit(solution)/shard_map/ppermute | solution.py:39
  (106 other events, 1084.6 us)
